TPU v7x, 256 devices: a whole 4x4x8 slice. The times are simulated.
256 devices in a mesh: member: 64 (over z, x, core), dp: 4 (over y).
Axes of the slice: x: 4, y: 4, z: 8, core: 2. Of those that a mesh axis runs over, the one named last changes fastest.
Arguments:
- feature_pool: bfloat16 [2048, 256], P('dp'), may hold values from -6 to 6
- labels: int32 [2048], P('dp'), may hold values from 0 to 9
- sample_rows: int32 [1024], P('dp'), may hold values from 0 to 511
- noise_variance: float32 [10], replicated, may hold values from 20 to 80
- first_weight: bfloat16 [128, 256, 2048], P('member', None, 'dp'), may hold values from -6 to 6
- middle_weight: bfloat16 [128, 2048, 2048], P('member', 'dp'), may hold values from -6 to 6
- last_weight: bfloat16 [128, 2048, 10], P('member', 'dp'), may hold values from -6 to 6
Outputs:
- new_first: bfloat16 [128, 256, 2048], P('member', None, 'dp')
- new_middle: bfloat16 [128, 2048, 2048], P('member', 'dp')
- new_last: bfloat16 [128, 2048, 10], P('member', 'dp')
Inputs may be any that keep to these rules, and one draw needn't show every extreme that they name: Sample i reads pool row (i // 256) * 512 + sample_rows[i]. `labels`: class index of each pool row.
All inputs are finite; a program needn't handle non-finite values.
Results may differ from a plain program's by a relative error of at most 0.013.
Values may be sent and summed in bfloat16 or wider, within the bound.
A program may use at most 128 MiB of HBM per device.

v0:
```python
import jax
import jax.numpy as jnp
from jax import lax
from jax.sharding import PartitionSpec as P

F_IN = 256
H = 2048
precise = lax.Precision.HIGHEST


def from_everyone(x, axis):
    size = lax.axis_size(axis)
    return lax.all_to_all(jnp.broadcast_to(x[None], (size, *x.shape)), axis, 0, 0, tiled=True)


def in_order(parts, dim):
    shape = list(parts.shape[1:])
    shape[dim] *= parts.shape[0]
    return jnp.moveaxis(parts, 0, dim).reshape(shape)


def gathered_copies(x, axis, dim):
    parts = from_everyone(x, axis)
    return in_order(parts, dim)


def side_by_side(arrays, axis, split_dim, concat_dim, along):
    widths = [a.shape[along] for a in arrays]
    both = jnp.concatenate(arrays, axis=along)
    filled = lax.all_to_all(both, axis, split_axis=split_dim, concat_axis=concat_dim, tiled=True)
    return tuple(jnp.split(filled, [sum(widths[:k]) for k in range(1, len(widths))], axis=along))


def update_piece(piece, mixing):
    ensemble = piece.shape[0]
    flat = piece.reshape(ensemble, -1)
    upper = mixing.astype(jnp.bfloat16)
    lower = (mixing - upper.astype(jnp.float32)).astype(jnp.bfloat16)
    stacked = jnp.concatenate([upper.T, lower.T], axis=0)
    both = jnp.dot(stacked, flat, preferred_element_type=jnp.float32)
    product = both[:ensemble] + both[ensemble:]
    column_total = jnp.sum(mixing, axis=0)
    average = jnp.sum(flat, axis=0, dtype=jnp.float32) / ensemble
    renewed = flat.astype(jnp.float32) + product - column_total[:, None] * average[None, :]
    return renewed.astype(jnp.bfloat16).reshape(piece.shape)


def on_device(
    feature_pool, labels, sample_rows, noise_variance, first_weight, middle_weight, last_weight
):
    local_count = sample_rows.shape[0]
    members_here = first_weight.shape[0]
    classes_total = noise_variance.shape[0]
    in_scale = F_IN ** (-0.5)
    hid_scale = H ** (-0.5)
    inputs = feature_pool[sample_rows]
    classes = labels[sample_rows]
    target = (classes[:, None] == jnp.arange(classes_total, dtype=jnp.int32)[None, :]).astype(
        jnp.float32
    )
    window = gathered_copies(inputs, "dp", 0)
    hidden_one = jnp.tanh(
        jnp.einsum("sf,jfh->jsh", window, first_weight, preferred_element_type=jnp.float32)
        * in_scale
    ).astype(jnp.bfloat16)
    term = jnp.einsum("jsk,jkh->sjh", hidden_one, middle_weight, preferred_element_type=jnp.float32)
    summed = lax.psum_scatter(
        term.reshape(lax.axis_size("dp") * local_count, members_here * H).astype(jnp.bfloat16),
        "dp",
        scatter_dimension=0,
        tiled=True,
    ).astype(jnp.float32)
    hidden_two = jnp.tanh(summed.reshape(local_count, members_here, H) * hid_scale).astype(
        jnp.bfloat16
    )
    last_full = lax.all_gather(last_weight, "dp", axis=1, tiled=True)
    outputs = (
        jnp.einsum("sjh,jhc->jsc", hidden_two, last_full, preferred_element_type=jnp.float32)
        * hid_scale
    )
    whiten = 1.0 / jnp.sqrt(noise_variance)
    scaled = (outputs * whiten).reshape(members_here, local_count * classes_total)
    observed = (target * whiten).reshape(local_count * classes_total)
    every_member = lax.all_gather(scaled, "member", axis=0, tiled=True)
    center = jnp.mean(every_member, axis=0)
    anomaly = every_member - center
    gram_part = jnp.dot(anomaly, anomaly.T, precision=precise)
    drive_part = jnp.dot(anomaly, observed - center, precision=precise)
    gram_matrix, drive = (
        lax.psum(gram_part.astype(jnp.bfloat16), "dp").astype(jnp.float32),
        lax.psum(drive_part.astype(jnp.bfloat16), "dp").astype(jnp.float32),
    )
    ensemble = gram_matrix.shape[0]
    system = gram_matrix + ensemble * jnp.eye(ensemble, dtype=jnp.float32)
    factor = jnp.linalg.cholesky(system)
    mixing = jax.scipy.linalg.cho_solve((factor, True), drive[:, None] - gram_matrix)
    grouped = (
        lax.all_to_all(first_weight, "member", split_axis=1, concat_axis=0, tiled=True),
        *side_by_side((middle_weight, last_weight), "member", 1, 0, 2),
    )
    updated = (
        update_piece(grouped[0], mixing),
        update_piece(grouped[1], mixing),
        update_piece(grouped[2], mixing),
    )
    new_first, new_middle, new_last = (
        lax.all_to_all(updated[0], "member", split_axis=0, concat_axis=1, tiled=True),
        *side_by_side((updated[1], updated[2]), "member", 0, 1, 2),
    )
    return (new_first, new_middle, new_last)


def solution(mesh):
    in_specs = (
        P("dp", None),
        P("dp"),
        P("dp"),
        P(),
        P("member", None, "dp"),
        P("member", "dp", None),
        P("member", "dp", None),
    )
    out_specs = (P("member", None, "dp"), P("member", "dp", None), P("member", "dp", None))
    return jax.shard_map(
        on_device, mesh=mesh, in_specs=in_specs, out_specs=out_specs, check_vma=False
    )
```

profile of v0, /device:TPU:2, one launch (start us, length us, event | category | flops | bytes accessed | tf_op | source)
XLA Modules:
  0.0 416.6 jit_solution(17062474247449413385)
XLA Ops:
  7.2 0.7 compare_select_fusion
  8.0 0.2 copy-done
  8.1 1.1 gather_fusion
  9.3 13.7 %all_to_all.74 = bf16[4,256,256]{2,1,0:T(8,128)(2,1)S(1)} all-to-all(bf16[4,256,256]{2,1,0:T(8,128)(2,1)S(1)} %broadcast_in_dim.6), channel_id=1, replica_groups=mesh['member'=64,'dp'=4] {'dp'}, dimensions={0} | all-to-all | bytes 1048576 | tf_op jit(solution)/shard_map/all_to_all | solution.py:13
  23.1 9.5 %convert_bitcast_fusion = bf16[1024,2,2048]{2,0,1:T(8,128)(2,1)} fusion(bf16[2,512,2048]{2,1,0:T(8,128)(2,1)} %param.12, bf16[1024,256,1]{1,0,2:T(8,128)(2,1)S(1)} %bitcast.96, bf16[2,256,512]{2,1,0:T(8,128)(2,1)} %param.11), kind=kOutput, calls=%fused_computation.7 | convolution fusion | flops 4838129664 | bytes 13631488 | tf_op jit(solution)/shard_map/jsk,jkh->sjh/dot_general | solution.py:66
  32.5 11.9 %copy.78 = bf16[1024,2,2048]{0,2,1:T(8,128)(2,1)} copy(bf16[1024,2,2048]{2,0,1:T(8,128)(2,1)} %convert_bitcast_fusion) | data formatting | bytes 16777216 | tf_op jit(solution)/shard_map/convert_element_type | solution.py:68
  44.4 1.0 copy-done.5
  45.4 1.3 copy.76
  46.8 12.4 %all-to-all-start = ((bf16[2,256,512]{2,0,1:T(2,128)(2,1)}), bf16[2,256,512]{2,0,1:T(2,128)(2,1)S(1)}, u32[]{:S(2)}, u32[]{:S(2)}) async-start(bf16[2,256,512]{2,0,1:T(2,128)(2,1)} %copy.76), calls=%async_computation | async-start | bytes 1048576 | tf_op jit(solution)/shard_map/all_to_all | solution.py:98
  59.2 8.5 %copy.84 = bf16[2,512,2048]{2,0,1:T(2,128)(2,1)} copy(bf16[2,512,2048]{2,1,0:T(8,128)(2,1)} %param.12) | data formatting | bytes 8388608 | tf_op args[5]
  67.7 0.2 copy.85
  67.9 8.4 %pad_maximum_fusion = bf16[2,512,2058]{2,0,1:T(2,128)(2,1)} fusion(bf16[2,512,10]{2,0,1:T(2,128)(2,1)S(1)} %copy.85, bf16[2,512,2048]{2,0,1:T(2,128)(2,1)} %copy.84), kind=kLoop, calls=%fused_computation.8 | loop fusion | flops 8429568 | bytes 8429568 | tf_op jit(solution)/shard_map/concatenate | solution.py:29
  76.3 0.3 all-to-all-done
  76.6 10.3 %all-to-all-start.3 = ((bf16[2,512,2058]{2,0,1:T(2,128)(2,1)}), bf16[2,512,2058]{2,0,1:T(2,128)(2,1)}, u32[]{:S(2)}, u32[]{:S(2)}) async-start(bf16[2,512,2058]{2,0,1:T(2,128)(2,1)} %pad_maximum_fusion), calls=%async_computation.4 | async-start | bytes 8912896 | tf_op jit(solution)/shard_map/all_to_all | solution.py:30
  87.0 13.2 %all_gather.6 = bf16[2,2048,10]{1,2,0:T(8,128)(2,1)S(1)} all-gather(bf16[2,512,10]{1,2,0:T(8,128)(2,1)S(1)} %copy.79), channel_id=1, replica_groups=mesh['member'=64,'dp'=4] {'dp'}, dimensions={1}, use_global_device_ids=true | all-gather | bytes 102400 | tf_op jit(solution)/shard_map/all_gather | solution.py:76
  100.1 29.5 %reduce-scatter.2.cloned.1.call-done = bf16[256,4096]{0,1:T(8,128)(2,1)} async-done(((bf16[1024,4096]{0,1:T(8,128)(2,1)}), bf16[256,4096]{0,1:T(8,128)(2,1)}) %reduce-scatter.2.cloned.1.call-update) | async-done | bytes 2097168 | tf_op jit(solution)/shard_map/reduce_scatter | solution.py:67
  129.6 2.1 tanh_convert_fusion
  131.8 0.3 convolution_multiply_fusion
  132.1 0.2 copy.81
  132.3 0.8 reshape.120
  133.1 1.9 gather_fusion.1
  135.1 0.1 fusion.22
  135.2 0.1 mul.95
  135.3 0.2 copy.77
  135.6 0.1 copy.93
  135.7 0.3 convert_reduce_fusion.1
  136.0 53.5 %all-to-all-done.3 = bf16[2,512,2058]{2,0,1:T(2,128)(2,1)} async-done(((bf16[2,512,2058]{2,0,1:T(2,128)(2,1)}), bf16[2,512,2058]{2,0,1:T(2,128)(2,1)}, u32[]{:S(2)}, u32[]{:S(2)}) %all-to-all-start.3) | async-done | bytes 4214816 | tf_op jit(solution)/shard_map/all_to_all | solution.py:30
  189.4 3.0 copy.86
  192.5 3.0 split.16
  195.5 0.4 copy-done.3
  195.8 0.1 convert_reduce_fusion.2
  196.1 2.8 convert_reduce_fusion
  198.9 0.2 reshape.126
  199.1 7.3 %copy.95 = bf16[16,8,8,2048]{3,1,2,0:T(8,128)(2,1)} copy(bf16[16,8,8,2048]{3,2,1,0:T(8,128)(2,1)} %bitcast.85) | data formatting | bytes 8388608
  206.5 11.1 %all-gather.3.cloned.1.call-done = f32[64,2,2560]{2,1,0:T(2,128)} async-done(((f32[1,2,2560]{2,1,0:T(2,128)}), f32[64,2,2560]{2,1,0:T(2,128)}) %all-gather.3.cloned.1.call-update) | async-done | bytes 1310736 | tf_op jit(solution)/shard_map/all_gather | solution.py:84
  217.7 1.7 reduce_sum.43
  219.4 2.2 reshape.121
  221.6 1.2 fusion.8
  222.8 1.1 fusion.14
  223.9 17.5 %all-reduce = (bf16[128,128]{1,0:T(8,128)(2,1)S(1)}, bf16[128]{0:T(256)(128)(2,1)S(1)}) all-reduce(bf16[128,128]{1,0:T(8,128)(2,1)S(1)} %fusion.8, bf16[128]{0:T(256)(128)(2,1)S(1)} %fusion.14), channel_id=1, replica_groups=mesh['member'=64,'dp'=4] {'dp'}, use_global_device_ids=true, to_apply=%region_2.0 | all-reduce | flops 16512 | bytes 66048 | tf_op jit(solution)/shard_map/psum | solution.py:90
  241.6 11.7 %cholesky.16 = f32[128,128]{1,0:T(8,128)S(1)} custom-call(f32[128,128]{1,0:T(8,128)S(1)} %fusion.29), custom_call_target="Cholesky" | custom-call | tf_op jit(solution)/shard_map/jit(cholesky)/cholesky | solution.py:95
  253.4 0.6 compare_reduce_fusion
  254.0 0.7 fusion.23
  254.7 9.8 %custom-call.10 = f32[1,128,128]{1,2,0:T(8,128)S(1)} custom-call(f32[1,128,128]{2,1,0:T(8,128)S(1)} %fusion.23), custom_call_target="InvertDiagBlocksLowerTriangular" | custom-call | tf_op jit(solution)/shard_map/jit(_cho_solve)/triangular_solve | solution.py:96
  264.5 0.3 fusion.24
  264.8 0.2 fusion.25
  265.0 0.4 fusion.36
  265.5 0.3 fusion.19
  265.8 1.2 reshape.97
  267.0 8.2 %all-to-all-start.2 = ((bf16[128,4,512]{2,1,0:T(4,128)(2,1)}), bf16[128,4,512]{2,1,0:T(4,128)(2,1)S(1)}, u32[]{:S(2)}, u32[]{:S(2)}) async-start(bf16[128,4,512]{2,1,0:T(4,128)(2,1)} %reshape.97), calls=%async_computation.3 | async-start | bytes 1048576 | tf_op jit(solution)/shard_map/all_to_all | solution.py:107
  275.2 4.7 %fusion.35 = f32[256,16384]{1,0:T(8,128)S(1)} fusion(bf16[128,16384]{1,0:T(8,128)(2,1)} %bitcast.80, bf16[128,128]{0,1:T(8,128)(2,1)S(1)} %get-tuple-element.29, bf16[128,128]{0,1:T(8,128)(2,1)S(1)} %get-tuple-element.24), kind=kOutput, calls=%fused_computation.57 | convolution fusion | flops 1073872896 | bytes 21037056 | tf_op jit(solution)/shard_map/dot_general | solution.py:40
  280.0 3.3 fusion.2
  283.3 0.2 fusion.34
  283.6 0.2 copy.88
  283.8 5.0 %copy.97 = bf16[16,8,8,2048]{3,2,1,0:T(8,128)(2,1)S(1)} copy(bf16[16,8,8,2048]{3,1,2,0:T(8,128)(2,1)} %bitcast.87) | data formatting | bytes 8388608
  288.8 2.5 pad_maximum_fusion.1
  291.3 1.3 all-to-all-done.2
  292.7 9.1 %all-to-all-start.4 = ((bf16[128,8,2058]{2,1,0:T(8,128)(2,1)}), bf16[128,8,2058]{2,1,0:T(8,128)(2,1)}, u32[]{:S(2)}, u32[]{:S(2)}) async-start(bf16[128,8,2058]{2,1,0:T(8,128)(2,1)} %pad_maximum_fusion.1), calls=%async_computation.5 | async-start | bytes 8912896 | tf_op jit(solution)/shard_map/all_to_all | solution.py:30
  301.8 0.2 copy.102
  302.0 0.9 all_to_all.60
  302.9 100.7 %all-to-all-done.4 = bf16[128,8,2058]{2,1,0:T(8,128)(2,1)} async-done(((bf16[128,8,2058]{2,1,0:T(8,128)(2,1)}), bf16[128,8,2058]{2,1,0:T(8,128)(2,1)}, u32[]{:S(2)}, u32[]{:S(2)}) %all-to-all-start.4) | async-done | bytes 4214816 | tf_op jit(solution)/shard_map/all_to_all | solution.py:30
  403.5 2.6 copy.101
  406.2 2.6 split.18
  408.8 0.8 copy.90
  (40 shorter events, 0.8 us)
Async XLA Ops:
  7.2 1.0 copy-start
  7.2 122.4 %reduce-scatter.2.cloned.1.call-start = ((), (), s32[]{:S(2)}) async-start(), calls=%async_computation.6 | async-start | bytes 10485760 | tf_op jit(solution)/shard_map/reduce_scatter | solution.py:67
  44.4 1.0 copy-start.5
  46.8 29.9 %all-to-all-start = ((bf16[2,256,512]{2,0,1:T(2,128)(2,1)}), bf16[2,256,512]{2,0,1:T(2,128)(2,1)S(1)}, u32[]{:S(2)}, u32[]{:S(2)}) async-start(bf16[2,256,512]{2,0,1:T(2,128)(2,1)} %copy.76), calls=%async_computation | async-start | bytes 1048576 | tf_op jit(solution)/shard_map/all_to_all | solution.py:98
  59.2 8.5 %copy-start.6 = (bf16[2,512,10]{1,0,2:T(2,128)(2,1)S(1)}, bf16[2,512,10]{1,0,2:T(2,128)(2,1)}, u32[]{:S(2)}) copy-start(bf16[2,512,10]{1,0,2:T(2,128)(2,1)} %param.13) | copy-start | bytes 61444
  76.3 23.8 %copy-start.7 = (f32[10]{0:T(128)S(1)}, f32[10]{0:T(128)}, u32[]{:S(2)}) copy-start(f32[10]{0:T(128)} %param.10) | copy-start | bytes 124
  76.6 112.8 %all-to-all-start.3 = ((bf16[2,512,2058]{2,0,1:T(2,128)(2,1)}), bf16[2,512,2058]{2,0,1:T(2,128)(2,1)}, u32[]{:S(2)}, u32[]{:S(2)}) async-start(bf16[2,512,2058]{2,0,1:T(2,128)(2,1)} %pad_maximum_fusion), calls=%async_computation.4 | async-start | bytes 8912896 | tf_op jit(solution)/shard_map/all_to_all | solution.py:30
  86.9 46.2 %copy-start.2 = (s32[512]{0:T(512)S(1)}, s32[512]{0:T(512)}, u32[]{:S(2)}) copy-start(s32[512]{0:T(512)} %param.8) | copy-start | bytes 6148
  86.9 130.7 %all-gather.3.cloned.1.call-start = ((), (), s32[]{:S(2)}) async-start(), calls=%async_computation.7 | async-start | bytes 1331200 | tf_op jit(solution)/shard_map/all_gather | solution.py:84
  192.5 3.4 copy-start.3
  267.0 25.7 %all-to-all-start.2 = ((bf16[128,4,512]{2,1,0:T(4,128)(2,1)}), bf16[128,4,512]{2,1,0:T(4,128)(2,1)S(1)}, u32[]{:S(2)}, u32[]{:S(2)}) async-start(bf16[128,4,512]{2,1,0:T(4,128)(2,1)} %reshape.97), calls=%async_computation.3 | async-start | bytes 1048576 | tf_op jit(solution)/shard_map/all_to_all | solution.py:107
  275.2 4.7 %copy-start.4 = (bf16[16,8,8,2048]{3,1,2,0:T(8,128)(2,1)S(1)}, bf16[16,8,8,2048]{3,1,2,0:T(8,128)(2,1)}, u32[]{:S(2)}) copy-start(bf16[16,8,8,2048]{3,1,2,0:T(8,128)(2,1)} %copy.95) | copy-start | bytes 12582916
  292.7 110.9 %all-to-all-start.4 = ((bf16[128,8,2058]{2,1,0:T(8,128)(2,1)}), bf16[128,8,2058]{2,1,0:T(8,128)(2,1)}, u32[]{:S(2)}, u32[]{:S(2)}) async-start(bf16[128,8,2058]{2,1,0:T(8,128)(2,1)} %pad_maximum_fusion.1), calls=%async_computation.5 | async-start | bytes 8912896 | tf_op jit(solution)/shard_map/all_to_all | solution.py:30
  406.1 3.4 copy-start.1
Sparse Core Ops, SparseCore 0:
  44.5 85.0 reduce-scatter.1
  133.2 84.3 all-gather.2
where the time goes:
time: 422 us; the launch traced here: 417 us
  waiting for transfers between devices  196 us (46%)
  local copies, waits for them, and re-layouts  57.5 us (14%)
  other arithmetic  45.5 us (11%)
  blocking collectives  44.4 us (11%)
  starting transfers between devices  40.1 us (10%)
  matrix products  18 us (4%)
  between operations  14.6 us (3%)
    all_to_all x2, waiting for transfers between devices, side_by_side(): lax.all_to_all(both, axis, split_axis=split_dim, concat_axis=concat_dim,...  154 us
    reduce_scatter x1, waiting for transfers between devices, on_device(): lax.psum_scatter(term.reshape(lax.axis_size('dp') * local_count, members_...  29.5 us
    unnamed x28, local copies, waits for them, and re-layouts  27.9 us
    all_to_all x2, starting transfers between devices, side_by_side(): lax.all_to_all(both, axis, split_axis=split_dim, concat_axis=concat_dim,...  19.4 us
    psum x1, blocking collectives, on_device(): lax.psum(gram_part.astype(jnp.bfloat16), 'dp').astype(jnp.float32)  17.5 us
    all_to_all x1, blocking collectives, from_everyone(): lax.all_to_all(jnp.broadcast_to(x[None], (size, *x.shape)), axis, 0, 0, t...  13.7 us
    all_gather x1, blocking collectives, on_device(): last_full = lax.all_gather(last_weight, 'dp', axis=1, tiled=True)  13.2 us
    all_to_all x1, starting transfers between devices, on_device(): lax.all_to_all(first_weight, 'member', split_axis=1, concat_axis=0, tiled...  12.4 us
  transfers between devices with their start and end apart: 6, of which 6 were waited for; matrix products, arithmetic and copies ran while one was open for 14% of the time, Pallas kernels for 0%

commit v1 on v0

--- a/solution.py
+++ b/solution.py
@@ -6,6 +6,32 @@
 F_IN = 256
 H = 2048
 precise = lax.Precision.HIGHEST
+
+
+def _open_run(base_x, along_axis, t0):
+    newest, side_arr, o_now = (
+        lax.axis_size(along_axis),
+        lax.axis_index(along_axis),
+        base_x.shape[1],
+    )
+    gallery = []
+    for p in [*range(newest)]:
+        gallery.append((p, (p + 1) % newest))
+    steps_seen = []
+    for p in tuple(range(newest)):
+        steps_seen.append((p, (p - 1) % newest))
+    next_value = newest // 2
+    state_next = x_now = base_x
+    near = t0(base_x, side_arr * o_now)
+    for hop_no in [*range(1, next_value + 1)]:
+        state_next = lax.ppermute(state_next, along_axis, gallery)
+        if hop_no < newest - next_value:
+            x_now = lax.ppermute(x_now, along_axis, steps_seen)
+            local_now = t0(x_now, (side_arr + hop_no) % newest * o_now)
+            near = near + local_now
+        b_next = t0(state_next, (side_arr - hop_no) % newest * o_now)
+        near = near + b_next
+    return near
 
 
 def from_everyone(x, axis):
@@ -73,9 +99,17 @@
     hidden_two = jnp.tanh(summed.reshape(local_count, members_here, H) * hid_scale).astype(
         jnp.bfloat16
     )
-    last_full = lax.all_gather(last_weight, "dp", axis=1, tiled=True)
     outputs = (
-        jnp.einsum("sjh,jhc->jsc", hidden_two, last_full, preferred_element_type=jnp.float32)
+        _open_run(
+            last_weight,
+            "dp",
+            lambda shard, at: jnp.einsum(
+                "sjh,jhc->jsc",
+                lax.dynamic_slice_in_dim(hidden_two, at, shard.shape[1], axis=2),
+                shard,
+                preferred_element_type=jnp.float32,
+            ),
+        )
         * hid_scale
     )
     whiten = 1.0 / jnp.sqrt(noise_variance)

time: 422 us -> 422 us (level)
  blocking collectives: 44.4 us -> 31.3 us
  waiting for transfers between devices: 196 us -> 207 us
    all_gather x1 -> x0, blocking collectives: 13.2 us -> none  [on_device(): last_full = lax.all_gather(last_weight, 'dp', axis=1, tiled=True)]
    reduce_scatter x1, waiting for transfers between devices: 29.5 us -> 35.4 us  [on_device(): lax.psum_scatter(term.reshape(lax.axis_size('dp') * local_count, members_...]
    ppermute x0 -> x3, waiting for transfers between devices: none -> 5.08 us  [the longest x2 5.07 us: _open_run(): state_next = lax.ppermute(state_next, along_axis, gallery)]
  transfers between devices with their start and end apart: 6 -> 9, of which waited for: 6 -> 7; matrix products, arithmetic and copies ran while one was open for 14% -> 14% of each run, Pallas kernels for 0% -> 0%
where the time goes in v1:
time: 422 us; the launch traced here: 417 us
  waiting for transfers between devices  207 us (49%)
  local copies, waits for them, and re-layouts  57.5 us (14%)
  other arithmetic  45.5 us (11%)
  starting transfers between devices  42.7 us (10%)
  blocking collectives  31.3 us (7%)
  matrix products  18.3 us (4%)
  between operations  14.7 us (3%)
    all_to_all x2, waiting for transfers between devices, side_by_side(): lax.all_to_all(both, axis, split_axis=split_dim, concat_axis=concat_dim,...  154 us
    reduce_scatter x1, waiting for transfers between devices, on_device(): lax.psum_scatter(term.reshape(lax.axis_size('dp') * local_count, members_...  35.4 us
    unnamed x28, local copies, waits for them, and re-layouts  27.8 us
    all_to_all x2, starting transfers between devices, side_by_side(): lax.all_to_all(both, axis, split_axis=split_dim, concat_axis=concat_dim,...  19.4 us
    psum x1, blocking collectives, on_device(): lax.psum(gram_part.astype(jnp.bfloat16), 'dp').astype(jnp.float32)  17.6 us
    all_to_all x1, blocking collectives, from_everyone(): lax.all_to_all(jnp.broadcast_to(x[None], (size, *x.shape)), axis, 0, 0, t...  13.7 us
    all_to_all x1, starting transfers between devices, on_device(): lax.all_to_all(first_weight, 'member', split_axis=1, concat_axis=0, tiled...  12.6 us
    another operation x3, other arithmetic, on_device(): factor = jnp.linalg.cholesky(system)  12.4 us
  transfers between devices with their start and end apart: 9, of which 7 were waited for; matrix products, arithmetic and copies ran while one was open for 14% of the time, Pallas kernels for 0%

profile of v1, /device:TPU:2, one launch (start us, length us, event | category | flops | bytes accessed | tf_op | source)
XLA Modules:
  0.0 416.9 jit_solution(664232557215063313)
XLA Ops:
  7.2 0.7 compare_select_fusion
  8.0 0.2 copy-done
  8.1 1.1 gather_fusion
  9.3 13.7 %all_to_all.74 = bf16[4,256,256]{2,1,0:T(8,128)(2,1)S(1)} all-to-all(bf16[4,256,256]{2,1,0:T(8,128)(2,1)S(1)} %broadcast_in_dim.6), channel_id=1, replica_groups=mesh['member'=64,'dp'=4] {'dp'}, dimensions={0} | all-to-all | bytes 1048576 | tf_op jit(solution)/shard_map/all_to_all | solution.py:39
  23.1 9.5 %convert_bitcast_fusion = bf16[1024,2,2048]{2,0,1:T(8,128)(2,1)} fusion(bf16[2,512,2048]{2,1,0:T(8,128)(2,1)} %param.12, bf16[1024,256,1]{1,0,2:T(8,128)(2,1)S(1)} %bitcast.100, bf16[2,256,512]{2,1,0:T(8,128)(2,1)} %param.11), kind=kOutput, calls=%fused_computation.7 | convolution fusion | flops 4838129664 | bytes 13631488 | tf_op jit(solution)/shard_map/jsk,jkh->sjh/dot_general | solution.py:92
  32.5 11.9 %copy.100 = bf16[1024,2,2048]{0,2,1:T(8,128)(2,1)} copy(bf16[1024,2,2048]{2,0,1:T(8,128)(2,1)} %convert_bitcast_fusion) | data formatting | bytes 16777216 | tf_op jit(solution)/shard_map/convert_element_type | solution.py:94
  44.4 1.0 copy-done.5
  45.4 1.3 copy.98
  46.8 12.6 %all-to-all-start = ((bf16[2,256,512]{2,0,1:T(2,128)(2,1)}), bf16[2,256,512]{2,0,1:T(2,128)(2,1)S(1)}, u32[]{:S(2)}, u32[]{:S(2)}) async-start(bf16[2,256,512]{2,0,1:T(2,128)(2,1)} %copy.98), calls=%async_computation | async-start | bytes 1048576 | tf_op jit(solution)/shard_map/all_to_all | solution.py:132
  59.4 8.5 %copy.111 = bf16[2,512,2048]{2,0,1:T(2,128)(2,1)} copy(bf16[2,512,2048]{2,1,0:T(8,128)(2,1)} %param.12) | data formatting | bytes 8388608 | tf_op args[5]
  68.0 0.2 copy.112
  68.2 8.4 %pad_maximum_fusion = bf16[2,512,2058]{2,0,1:T(2,128)(2,1)} fusion(bf16[2,512,10]{2,0,1:T(2,128)(2,1)S(1)} %copy.112, bf16[2,512,2048]{2,0,1:T(2,128)(2,1)} %copy.111), kind=kLoop, calls=%fused_computation.8 | loop fusion | flops 8429568 | bytes 8429568 | tf_op jit(solution)/shard_map/concatenate | solution.py:55
  76.6 0.3 all-to-all-done
  76.9 10.3 %all-to-all-start.3 = ((bf16[2,512,2058]{2,0,1:T(2,128)(2,1)}), bf16[2,512,2058]{2,0,1:T(2,128)(2,1)}, u32[]{:S(2)}, u32[]{:S(2)}) async-start(bf16[2,512,2058]{2,0,1:T(2,128)(2,1)} %pad_maximum_fusion), calls=%async_computation.4 | async-start | bytes 8912896 | tf_op jit(solution)/shard_map/all_to_all | solution.py:56
  87.2 1.3 collective-permute-start
  88.5 0.8 collective-permute-start.1
  89.3 5.1 %collective-permute-done.1 = bf16[2,512,10]{1,2,0:T(8,128)(2,1)S(1)} collective-permute-done((bf16[2,512,10]{1,2,0:T(8,128)(2,1)S(1)}, bf16[2,512,10]{1,2,0:T(8,128)(2,1)S(1)}, u32[]{:S(2)}, u32[]{:S(2)}) %collective-permute-start.1) | collective-permute-done | bytes 20512 | tf_op jit(solution)/shard_map/ppermute | solution.py:27
  94.6 35.4 %reduce-scatter.2.cloned.1.call-done = bf16[256,4096]{0,1:T(8,128)(2,1)} async-done(((bf16[1024,4096]{0,1:T(8,128)(2,1)}), bf16[256,4096]{0,1:T(8,128)(2,1)}) %reduce-scatter.2.cloned.1.call-update) | async-done | bytes 2097168 | tf_op jit(solution)/shard_map/reduce_scatter | solution.py:93
  130.0 2.1 tanh_convert_fusion
  132.1 0.2 fusion.26
  132.3 0.2 convolution_add_fusion.2
  132.5 0.2 convolution_add_fusion.1
  132.8 0.2 copy.108
  133.0 0.8 reshape.120
  133.9 1.9 gather_fusion.1
  136.1 0.2 copy.99
  136.4 0.3 convert_reduce_fusion.1
  136.7 53.0 %all-to-all-done.3 = bf16[2,512,2058]{2,0,1:T(2,128)(2,1)} async-done(((bf16[2,512,2058]{2,0,1:T(2,128)(2,1)}), bf16[2,512,2058]{2,0,1:T(2,128)(2,1)}, u32[]{:S(2)}, u32[]{:S(2)}) %all-to-all-start.3) | async-done | bytes 4214816 | tf_op jit(solution)/shard_map/all_to_all | solution.py:56
  189.7 3.0 copy.113
  192.7 3.0 split.16
  195.7 0.4 copy-done.3
  196.3 2.8 convert_reduce_fusion
  199.1 0.2 reshape.126
  199.3 7.3 %copy.125 = bf16[16,8,8,2048]{3,1,2,0:T(8,128)(2,1)} copy(bf16[16,8,8,2048]{3,2,1,0:T(8,128)(2,1)} %bitcast.86) | data formatting | bytes 8388608
  206.8 11.1 %all-gather.3.cloned.1.call-done = f32[64,2,2560]{2,1,0:T(2,128)} async-done(((f32[1,2,2560]{2,1,0:T(2,128)}), f32[64,2,2560]{2,1,0:T(2,128)}) %all-gather.3.cloned.1.call-update) | async-done | bytes 1310736 | tf_op jit(solution)/shard_map/all_gather | solution.py:118
  217.8 1.7 reduce_sum.43
  219.6 2.2 reshape.121
  221.8 1.2 fusion.8
  223.0 1.1 fusion.15
  224.1 17.6 %all-reduce = (bf16[128,128]{1,0:T(8,128)(2,1)S(1)}, bf16[128]{0:T(256)(128)(2,1)S(1)}) all-reduce(bf16[128,128]{1,0:T(8,128)(2,1)S(1)} %fusion.8, bf16[128]{0:T(256)(128)(2,1)S(1)} %fusion.15), channel_id=1, replica_groups=mesh['member'=64,'dp'=4] {'dp'}, use_global_device_ids=true, to_apply=%region_2.3 | all-reduce | flops 16512 | bytes 66048 | tf_op jit(solution)/shard_map/psum | solution.py:124
  241.8 11.7 %cholesky.16 = f32[128,128]{1,0:T(8,128)S(1)} custom-call(f32[128,128]{1,0:T(8,128)S(1)} %fusion.35), custom_call_target="Cholesky" | custom-call | tf_op jit(solution)/shard_map/jit(cholesky)/cholesky | solution.py:129
  253.6 0.6 compare_reduce_fusion
  254.2 0.7 fusion.29
  254.9 9.8 %custom-call.10 = f32[1,128,128]{1,2,0:T(8,128)S(1)} custom-call(f32[1,128,128]{2,1,0:T(8,128)S(1)} %fusion.29), custom_call_target="InvertDiagBlocksLowerTriangular" | custom-call | tf_op jit(solution)/shard_map/jit(_cho_solve)/triangular_solve | solution.py:130
  264.7 0.3 fusion.30
  265.0 0.2 fusion.31
  265.3 0.4 fusion.42
  265.7 0.3 fusion.20
  266.0 1.2 reshape.97
  267.2 8.3 %all-to-all-start.2 = ((bf16[128,4,512]{2,1,0:T(4,128)(2,1)}), bf16[128,4,512]{2,1,0:T(4,128)(2,1)S(1)}, u32[]{:S(2)}, u32[]{:S(2)}) async-start(bf16[128,4,512]{2,1,0:T(4,128)(2,1)} %reshape.97), calls=%async_computation.3 | async-start | bytes 1048576 | tf_op jit(solution)/shard_map/all_to_all | solution.py:141
  275.5 4.7 %fusion.41 = f32[256,16384]{1,0:T(8,128)S(1)} fusion(bf16[128,16384]{1,0:T(8,128)(2,1)} %bitcast.81, bf16[128,128]{0,1:T(8,128)(2,1)S(1)} %get-tuple-element.29, bf16[128,128]{0,1:T(8,128)(2,1)S(1)} %get-tuple-element.24), kind=kOutput, calls=%fused_computation.65 | convolution fusion | flops 1073872896 | bytes 21037056 | tf_op jit(solution)/shard_map/dot_general | solution.py:66
  280.2 3.3 fusion.2
  283.5 0.2 fusion.40
  283.8 0.2 copy.115
  284.0 5.0 %copy.127 = bf16[16,8,8,2048]{3,2,1,0:T(8,128)(2,1)S(1)} copy(bf16[16,8,8,2048]{3,1,2,0:T(8,128)(2,1)} %bitcast.88) | data formatting | bytes 8388608
  289.0 2.5 pad_maximum_fusion.1
  291.6 1.3 all-to-all-done.2
  292.9 9.1 %all-to-all-start.4 = ((bf16[128,8,2058]{2,1,0:T(8,128)(2,1)}), bf16[128,8,2058]{2,1,0:T(8,128)(2,1)}, u32[]{:S(2)}, u32[]{:S(2)}) async-start(bf16[128,8,2058]{2,1,0:T(8,128)(2,1)} %pad_maximum_fusion.1), calls=%async_computation.5 | async-start | bytes 8912896 | tf_op jit(solution)/shard_map/all_to_all | solution.py:56
  302.0 0.2 copy.134
  302.2 0.9 all_to_all.60
  303.1 100.7 %all-to-all-done.4 = bf16[128,8,2058]{2,1,0:T(8,128)(2,1)} async-done(((bf16[128,8,2058]{2,1,0:T(8,128)(2,1)}), bf16[128,8,2058]{2,1,0:T(8,128)(2,1)}, u32[]{:S(2)}, u32[]{:S(2)}) %all-to-all-start.4) | async-done | bytes 4214816 | tf_op jit(solution)/shard_map/all_to_all | solution.py:56
  403.8 2.6 copy.133
  406.4 2.6 split.18
  409.0 0.8 copy.117
  (48 shorter events, 1.6 us)
Async XLA Ops:
  7.2 1.0 copy-start
  7.2 122.8 %reduce-scatter.2.cloned.1.call-start = ((), (), s32[]{:S(2)}) async-start(), calls=%async_computation.6 | async-start | bytes 10485760 | tf_op jit(solution)/shard_map/reduce_scatter | solution.py:93
  44.4 1.0 copy-start.5
  46.8 30.1 %all-to-all-start = ((bf16[2,256,512]{2,0,1:T(2,128)(2,1)}), bf16[2,256,512]{2,0,1:T(2,128)(2,1)S(1)}, u32[]{:S(2)}, u32[]{:S(2)}) async-start(bf16[2,256,512]{2,0,1:T(2,128)(2,1)} %copy.98), calls=%async_computation | async-start | bytes 1048576 | tf_op jit(solution)/shard_map/all_to_all | solution.py:132
  59.4 8.5 %copy-start.6 = (bf16[2,512,10]{1,0,2:T(2,128)(2,1)S(1)}, bf16[2,512,10]{1,0,2:T(2,128)(2,1)}, u32[]{:S(2)}) copy-start(bf16[2,512,10]{1,0,2:T(2,128)(2,1)} %param.13) | copy-start | bytes 61444
  76.6 12.8 %copy-start.7 = (f32[10]{0:T(128)S(1)}, f32[10]{0:T(128)}, u32[]{:S(2)}) copy-start(f32[10]{0:T(128)} %param.10) | copy-start | bytes 124
  76.9 112.8 %all-to-all-start.3 = ((bf16[2,512,2058]{2,0,1:T(2,128)(2,1)}), bf16[2,512,2058]{2,0,1:T(2,128)(2,1)}, u32[]{:S(2)}, u32[]{:S(2)}) async-start(bf16[2,512,2058]{2,0,1:T(2,128)(2,1)} %pad_maximum_fusion), calls=%async_computation.4 | async-start | bytes 8912896 | tf_op jit(solution)/shard_map/all_to_all | solution.py:56
  87.2 46.7 %copy-start.2 = (s32[512]{0:T(512)S(1)}, s32[512]{0:T(512)}, u32[]{:S(2)}) copy-start(s32[512]{0:T(512)} %param.8) | copy-start | bytes 6148
  87.2 130.7 %all-gather.3.cloned.1.call-start = ((), (), s32[]{:S(2)}) async-start(), calls=%async_computation.7 | async-start | bytes 1331200 | tf_op jit(solution)/shard_map/all_gather | solution.py:118
  87.2 45.1 %collective-permute-start = (bf16[2,512,10]{1,2,0:T(8,128)(2,1)S(1)}, bf16[2,512,10]{1,2,0:T(8,128)(2,1)S(1)}, u32[]{:S(2)}, u32[]{:S(2)}) collective-permute-start(bf16[2,512,10]{1,2,0:T(8,128)(2,1)S(1)} %copy.102), channel_id=1, source_target_pairs={{0,3},{1,0},{2,1},{3,2},{4,7},{5,4},{6,5},{7,6},{8,11},{9,8},{10,9... | collective-permute-start | bytes 61448 | tf_op jit(solution)/shard_map/ppermute | solution.py:29
  88.5 5.9 %collective-permute-start.1 = (bf16[2,512,10]{1,2,0:T(8,128)(2,1)S(1)}, bf16[2,512,10]{1,2,0:T(8,128)(2,1)S(1)}, u32[]{:S(2)}, u32[]{:S(2)}) collective-permute-start(bf16[2,512,10]{1,2,0:T(8,128)(2,1)S(1)} %copy.102), channel_id=1, source_target_pairs={{0,1},{1,2},{2,3},{3,0},{4,5},{5,6},{6,7},{7,4},{8,9},{9,10},{10,1... | collective-permute-start | bytes 61448 | tf_op jit(solution)/shard_map/ppermute | solution.py:27
  94.4 38.3 %collective-permute-start.2 = (bf16[2,512,10]{1,2,0:T(8,128)(2,1)S(1)}, bf16[2,512,10]{1,2,0:T(8,128)(2,1)S(1)}, u32[]{:S(2)}, u32[]{:S(2)}) collective-permute-start(bf16[2,512,10]{1,2,0:T(8,128)(2,1)S(1)} %collective-permute-done.1), channel_id=1, source_target_pairs={{0,1},{1,2},{2,3},{3,0},{4,5},{5,6},{6,7},{7,4},{8,9},{9,10},{10,1... | collective-permute-start | bytes 61448 | tf_op jit(solution)/shard_map/ppermute | solution.py:27
  192.7 3.4 copy-start.3
  267.2 25.7 %all-to-all-start.2 = ((bf16[128,4,512]{2,1,0:T(4,128)(2,1)}), bf16[128,4,512]{2,1,0:T(4,128)(2,1)S(1)}, u32[]{:S(2)}, u32[]{:S(2)}) async-start(bf16[128,4,512]{2,1,0:T(4,128)(2,1)} %reshape.97), calls=%async_computation.3 | async-start | bytes 1048576 | tf_op jit(solution)/shard_map/all_to_all | solution.py:141
  275.5 4.7 %copy-start.4 = (bf16[16,8,8,2048]{3,1,2,0:T(8,128)(2,1)S(1)}, bf16[16,8,8,2048]{3,1,2,0:T(8,128)(2,1)}, u32[]{:S(2)}) copy-start(bf16[16,8,8,2048]{3,1,2,0:T(8,128)(2,1)} %copy.125) | copy-start | bytes 12582916
  292.9 110.9 %all-to-all-start.4 = ((bf16[128,8,2058]{2,1,0:T(8,128)(2,1)}), bf16[128,8,2058]{2,1,0:T(8,128)(2,1)}, u32[]{:S(2)}, u32[]{:S(2)}) async-start(bf16[128,8,2058]{2,1,0:T(8,128)(2,1)} %pad_maximum_fusion.1), calls=%async_computation.5 | async-start | bytes 8912896 | tf_op jit(solution)/shard_map/all_to_all | solution.py:56
  406.4 3.4 copy-start.1
Sparse Core Ops, SparseCore 0:
  44.5 85.3 reduce-scatter.1
  134.0 83.8 all-gather.2
